TPU v7x, 512 devices: a whole 4x8x8 slice. The times are simulated.
512 devices in a mesh: hours: 64 (over z, x, core), region: 8 (over y).
Axes of the slice: x: 4, y: 8, z: 8, core: 2. Of those that a mesh axis runs over, the one named last changes fastest.
Arguments:
- availability: float32 [4096, 16, 1024], P('hours', None, 'region'), may hold values from 0.1 to 1
- demand: float32 [4096, 1024], P('hours', 'region'), may hold values from 2 to 72, as said below
- gen_cost: float32 [16, 1024], P(None, 'region'), may hold values from 0.05 to 1
- cap_cost: float32 [8, 2048], P('region', 'hours'), may hold values from 204.8 to 2048
- owner_map: int32 [8, 2048], P('region'), may hold values from 0 to 2047, each once within a row
- line_ends: int32 [2, 2048], P(None, 'region'), may hold values from 0 to 127
- line_limit: float32 [2048], P('region'), may hold values from 0.5 to 4
- cross_ends: int32 [2, 8, 256], P(None, 'region'), may hold values from 0 to 127
- cross_limit: float32 [8, 256], P('region'), may hold values from 0.5 to 4
- pair_counts: int32 [8, 8], P('region'), may hold values from 0 to 32, as said below
- store_node: int32 [2048], P('region'), may hold values from 0 to 127
- store_energy: float32 [2048], P('region'), may hold values from 0.02 to 0.4
- store_power: float32 [2048], P('region'), may hold values from 0.2 to 2
- price_start: float32 [4096, 1024], P('hours', 'region'), may hold values from -3 to 0.5
Outputs:
- dispatch: float32 [4096, 16, 1024], P('hours', None, 'region')
- capacity: float32 [8, 2048], P('region', 'hours')
- prices: float32 [4096, 1024], P('hours', 'region')
- charge_state: float32 [4096, 2048], P('hours', 'region')
Inputs may be any that keep to these rules, and one draw needn't show every extreme that they name: `demand`: loads are positive. `owner_map`: each row lists every capacity column of its region once. `pair_counts`: cross lines in use among the 32 slots of each ordered pair of regions; a region has none to itself; some pair uses all 32.
All inputs are finite; a program needn't handle non-finite values.
Results may differ from a plain program's by a relative error of at most 0.00018.
Values sent between devices are 32-bit elements; how exact they have to be, the bound alone decides.
A program may use at most 64 MiB of HBM per device.

v0:
```python
import jax
import jax.numpy as jnp
from jax import lax
from jax.sharding import PartitionSpec as P

ITERS = 4
epsilon = 1e-06
highest = lax.Precision.HIGHEST


def shifted(value, axis, steps):
    count = lax.axis_size(axis)
    pairs = [(source, (source + steps) % count) for source in range(count)]
    return lax.ppermute(value, axis, pairs)


def one_hot(indices, labels):
    return (indices[:, None] == labels[None, :]).astype(jnp.float32)


def to_owners(partial_value, owned_cols):
    summed = lax.psum(partial_value, "hours")
    return lax.dynamic_slice_in_dim(summed, lax.axis_index("hours") * owned_cols, owned_cols)


def spread_columns(capacity_bar):
    return lax.all_gather(capacity_bar, "hours", axis=0, tiled=True)


def body(
    availability,
    demand,
    gen_cost,
    cap_cost,
    owner_map,
    line_ends,
    line_limit,
    cross_ends,
    cross_limit,
    pair_counts,
    store_node,
    store_energy,
    store_power,
    price_start,
):
    hour_rows, tech_count, node_count = availability.shape
    region_count = lax.axis_size("region")
    slot_count = cross_limit.shape[1]
    slot_width = slot_count // region_count
    owned_cols = cap_cost.shape[1]
    owner_cols = owner_map[0]
    inverse = jnp.argsort(owner_cols)
    node_ids = jnp.arange(node_count, dtype=jnp.int32)
    line_inc = one_hot(line_ends[1], node_ids) - one_hot(line_ends[0], node_ids)
    store_map = one_hot(store_node, node_ids)
    leave_map = one_hot(cross_ends[0, 0], node_ids)
    slot_ids = jnp.arange(slot_count, dtype=jnp.int32)
    pair_of = slot_ids // slot_width
    region_ids = jnp.arange(region_count, dtype=jnp.int32)
    in_use = jnp.sum(
        jnp.where(pair_of[:, None] == region_ids[None, :], pair_counts[0][None, :], 0), axis=1
    )
    cross_bound = jnp.where(slot_ids % slot_width < in_use, cross_limit[0], 0.0)
    reach_map = one_hot(
        pair_of * node_count + cross_ends[1, 0],
        jnp.arange(region_count * node_count, dtype=jnp.int32),
    )
    column_costs = cap_cost[0]
    col_weight = to_owners(jnp.sum(availability, axis=0).reshape(-1)[owner_cols], owned_cols)
    dispatch = jnp.zeros_like(availability)
    capacity = jnp.zeros((owned_cols,), jnp.float32)
    inner_flow = jnp.zeros((hour_rows, line_limit.shape[0]), jnp.float32)
    cross_flow = jnp.zeros((hour_rows, slot_count), jnp.float32)
    mirror_flow = jnp.zeros((hour_rows, slot_count), jnp.float32)
    discharge = jnp.zeros((hour_rows, store_node.shape[0]), jnp.float32)
    charge = jnp.zeros((hour_rows, store_node.shape[0]), jnp.float32)
    prices = price_start
    cap_duals = jnp.zeros_like(availability)
    store_duals = jnp.zeros((hour_rows, store_node.shape[0]), jnp.float32)
    weight = jnp.float32(1.0)
    for iteration in range(ITERS):
        final_sweep = iteration == ITERS - 1
        primal_step = 0.5 / weight
        far_side = jnp.dot(
            lax.all_gather(prices, "region", axis=1, tiled=True), reach_map.T, precision=highest
        )
        if iteration == 0:
            next_duals = jnp.zeros_like(store_duals)
            cap_pull = jnp.zeros((owned_cols,), jnp.float32)
        else:
            next_row = shifted(store_duals[:1], "hours", -1)
            next_duals = jnp.concatenate([store_duals[1:], next_row], axis=0)
            cap_pull = to_owners(
                jnp.sum(availability * cap_duals, axis=0).reshape(-1)[owner_cols], owned_cols
            )
        dispatch_new = jnp.maximum(
            dispatch - primal_step * (gen_cost[None] + prices[:, None, :] + cap_duals), 0.0
        )
        capacity_new = jnp.maximum(
            capacity - (column_costs - cap_pull) / (weight * col_weight), 0.0
        )
        inner_new = jnp.clip(
            inner_flow - primal_step * jnp.dot(prices, line_inc.T, precision=highest),
            -line_limit,
            line_limit,
        )
        cross_new = jnp.clip(
            cross_flow - primal_step * (far_side - jnp.dot(prices, leave_map.T, precision=highest)),
            -cross_bound,
            cross_bound,
        )
        mirror_new = mirror_flow
        discharge_new = jnp.clip(
            discharge
            - primal_step * (jnp.dot(prices, store_map.T, precision=highest) + store_duals),
            -store_power,
            store_power,
        )
        charge_new = jnp.clip(charge - primal_step * (store_duals - next_duals), 0.0, store_energy)
        if not final_sweep:
            cap_change = capacity_new - capacity
            primal_sq = (
                jnp.sum((dispatch_new - dispatch) ** 2)
                + jnp.sum(cap_change**2)
                + jnp.sum((inner_new - inner_flow) ** 2)
                + jnp.sum((cross_new - cross_flow) ** 2)
                + jnp.sum((discharge_new - discharge) ** 2)
                + jnp.sum((charge_new - charge) ** 2)
            )
            primal_sum = lax.psum(primal_sq, ("hours", "region"))
        dispatch_bar = 2.0 * dispatch_new - dispatch
        capacity_bar = 2.0 * capacity_new - capacity
        inner_bar = 2.0 * inner_new - inner_flow
        cross_bar = 2.0 * cross_new - cross_flow
        discharge_bar = 2.0 * discharge_new - discharge
        charge_bar = 2.0 * charge_new - charge
        capacity_all = spread_columns(capacity_bar)
        cap_dense = capacity_all[inverse].reshape(tech_count, node_count)
        per_dest = jnp.dot(cross_bar, reach_map, precision=highest)
        balance = (
            jnp.sum(dispatch_bar, axis=1)
            + jnp.dot(inner_bar, line_inc, precision=highest)
            + (
                lax.psum_scatter(per_dest, "region", scatter_dimension=1, tiled=True)
                - jnp.dot(cross_bar, leave_map, precision=highest)
            )
            + jnp.dot(discharge_bar, store_map, precision=highest)
            - demand
        )
        prev_row = shifted(charge_bar[-1:], "hours", 1)
        storage_rows = (
            charge_bar - jnp.concatenate([prev_row, charge_bar[:-1]], axis=0) + discharge_bar
        )
        cap_rows = dispatch_bar - availability * cap_dense[None]
        prices_new = prices + weight / (tech_count + 8.0) * balance
        cap_new = jnp.maximum(cap_duals + weight / 2.0 * cap_rows, 0.0)
        store_new = store_duals + weight / 3.0 * storage_rows
        if not final_sweep:
            dual_sq = (
                jnp.sum((prices_new - prices) ** 2)
                + jnp.sum((cap_new - cap_duals) ** 2)
                + jnp.sum((store_new - store_duals) ** 2)
            )
            dual_sum = lax.psum(dual_sq, ("hours", "region"))
            weight = jnp.sqrt(weight * jnp.sqrt((dual_sum + epsilon) / (primal_sum + epsilon)))
        dispatch, capacity, inner_flow, cross_flow = (
            dispatch_new,
            capacity_new,
            inner_new,
            cross_new,
        )
        mirror_flow = mirror_new
        discharge, charge = (discharge_new, charge_new)
        prices, cap_duals, store_duals = (prices_new, cap_new, store_new)
    return (dispatch, capacity[None], prices, charge)


def solution(mesh):
    placed = (
        P("hours", None, "region"),
        P("hours", "region"),
        P(None, "region"),
        P("region", "hours"),
        P("region", None),
        P(None, "region"),
        P("region"),
        P(None, "region", None),
        P("region", None),
        P("region", None),
        P("region"),
        P("region"),
        P("region"),
        P("hours", "region"),
    )
    return jax.shard_map(
        body,
        mesh=mesh,
        in_specs=placed,
        out_specs=(
            P("hours", None, "region"),
            P("region", "hours"),
            P("hours", "region"),
            P("hours", "region"),
        ),
        check_vma=False,
    )
```

profile of v0, /device:TPU:2, one launch (start us, length us, event | category | flops | bytes accessed | tf_op | source)
XLA Modules:
  0.0 1496.5 jit_solution(16780039333863139814)
XLA Ops:
  7.2 0.7 broadcast_minimum_fusion
  7.9 2.0 collective-permute-start
  10.0 26.6 %all_gather.21 = f32[64,1024]{1,0:T(8,128)S(1)} all-gather(f32[64,128]{1,0:T(8,128)} %param.27), channel_id=1, replica_groups=mesh['hours'=64,'region'=8] {'region'}, dimensions={1}, use_global_device_ids=true | all-gather | bytes 294912 | tf_op jit(solution)/shard_map/all_gather | solution.py:85
  37.3 0.7 fusion.75
  38.1 0.9 multiply_reduce_fusion.20
  39.0 1.3 fusion.74
  41.2 11.8 gather_fusion
  53.0 126.8 %psum.70 = f32[2048]{0:T(1024)S(1)} all-reduce(f32[2048]{0:T(1024)S(1)} %gather_fusion), channel_id=1, replica_groups=mesh['hours'=64,'region'=8] {'hours'}, use_global_device_ids=true, to_apply=%region_5.6 | all-reduce | flops 2048 | bytes 16384 | tf_op jit(solution)/shard_map/psum | solution.py:22
  179.7 1.3 dynamic-slice
  181.7 0.7 multiply_reduce_fusion.28
  182.5 126.4 %all-reduce = f32[2048]{0:T(1024)S(1)} all-reduce(f32[2048]{0:T(1024)S(1)} %multiply_dynamic-update-slice_fusion), channel_id=1, replica_groups=mesh['hours'=64,'region'=8] {'hours'}, use_global_device_ids=true, to_apply=%add | all-reduce | flops 2048 | bytes 16384
  308.9 5.0 sort.17
  314.0 11.8 gather_fusion.1
  325.8 1.1 multiply_reduce_fusion.6
  326.8 11.8 gather_fusion.2
  338.6 1.0 multiply_reduce_fusion.21
  339.6 0.7 broadcast_reduce_fusion
  340.6 126.1 %psum.73 = f32[2048]{0:T(1024)S(1)} all-reduce(f32[2048]{0:T(1024)S(1)} %gather_fusion.2), channel_id=1, replica_groups=mesh['hours'=64,'region'=8] {'hours'}, use_global_device_ids=true, to_apply=%region_21.22 | all-reduce | flops 2048 | bytes 16384 | tf_op jit(solution)/shard_map/psum | solution.py:22
  469.9 0.9 multiply_reduce_fusion.19
  472.2 1.0 fusion.67
  473.2 0.9 multiply_reduce_fusion.25
  476.0 7.0 collective-permute-start.1
  483.0 95.3 %all-reduce.5 = (f32[]{:T(128)}, f32[]{:T(128)}) all-reduce(f32[]{:T(128)S(6)} %add.309, f32[]{:T(128)S(6)} %add.315), channel_id=1, replica_groups=mesh['hours'=64,'region'=8] {'hours','region'}, use_global_device_ids=true, to_apply=%region_9.10 | all-reduce | flops 2 | bytes 16 | tf_op jit(solution)/shard_map/psum | solution.py:164
  579.7 24.8 %all_gather.23 = f32[64,1024]{1,0:T(8,128)S(1)} all-gather(f32[64,128]{1,0:T(8,128)S(1)} %get-tuple-element.56), channel_id=1, replica_groups=mesh['hours'=64,'region'=8] {'region'}, dimensions={1}, use_global_device_ids=true | all-gather | bytes 294912 | tf_op jit(solution)/shard_map/all_gather | solution.py:85
  604.5 1.0 multiply_reduce_fusion.17
  605.6 0.7 multiply_reduce_fusion.27
  606.4 120.4 %all-reduce.1 = f32[2048]{0:T(1024)S(1)} all-reduce(f32[2048]{0:T(1024)S(1)} %subtract_dynamic-update-slice_fusion.1), channel_id=1, replica_groups=mesh['hours'=64,'region'=8] {'hours'}, use_global_device_ids=true, to_apply=%add.1 | all-reduce | flops 2048 | bytes 16384
  726.8 11.8 gather_fusion.3
  739.9 0.7 fusion.73
  740.7 0.9 multiply_reduce_fusion.16
  741.6 1.3 fusion.72
  742.9 1.2 multiply_reduce_fusion.3
  744.2 11.8 gather_fusion.4
  756.0 1.9 collective-permute-start.2
  758.2 131.1 %psum.76 = f32[2048]{0:T(1024)S(1)} all-reduce(f32[2048]{0:T(1024)S(1)} %gather_fusion.4), channel_id=1, replica_groups=mesh['hours'=64,'region'=8] {'hours'}, use_global_device_ids=true, to_apply=%region_36.37 | all-reduce | flops 2048 | bytes 16384 | tf_op jit(solution)/shard_map/psum | solution.py:22
  891.9 1.0 multiply_reduce_fusion.15
  894.2 1.0 fusion.63
  895.2 0.9 multiply_reduce_fusion.24
  898.0 1.9 collective-permute-start.3
  900.0 100.8 %all-reduce.4 = (f32[]{:T(128)}, f32[]{:T(128)}) all-reduce(f32[]{:T(128)S(6)} %add.329, f32[]{:T(128)S(6)} %add.335), channel_id=1, replica_groups=mesh['hours'=64,'region'=8] {'hours','region'}, use_global_device_ids=true, to_apply=%region_24.25 | all-reduce | flops 2 | bytes 16 | tf_op jit(solution)/shard_map/psum | solution.py:164
  1002.2 0.7 multiply_reduce_fusion.26
  1002.9 1.0 multiply_reduce_fusion.12
  1003.9 24.8 %all_gather.25 = f32[64,1024]{1,0:T(8,128)S(1)} all-gather(f32[64,128]{1,0:T(8,128)S(1)} %get-tuple-element.63), channel_id=1, replica_groups=mesh['hours'=64,'region'=8] {'region'}, dimensions={1}, use_global_device_ids=true | all-gather | bytes 294912 | tf_op jit(solution)/shard_map/all_gather | solution.py:85
  1029.5 120.4 %all-reduce.2 = f32[2048]{0:T(1024)S(1)} all-reduce(f32[2048]{0:T(1024)S(1)} %subtract_dynamic-update-slice_fusion), channel_id=1, replica_groups=mesh['hours'=64,'region'=8] {'hours'}, use_global_device_ids=true, to_apply=%add.2 | all-reduce | flops 2048 | bytes 16384
  1149.9 11.8 gather_fusion.5
  1161.7 1.9 collective-permute-start.4
  1163.7 0.7 fusion.71
  1164.4 0.9 multiply_reduce_fusion.11
  1165.3 1.3 fusion.70
  1166.7 1.4 multiply_reduce_fusion
  1168.1 11.8 gather_fusion.6
  1180.2 131.1 %psum.79 = f32[2048]{0:T(1024)S(1)} all-reduce(f32[2048]{0:T(1024)S(1)} %gather_fusion.6), channel_id=1, replica_groups=mesh['hours'=64,'region'=8] {'hours'}, use_global_device_ids=true, to_apply=%region_48.49 | all-reduce | flops 2048 | bytes 16384 | tf_op jit(solution)/shard_map/psum | solution.py:22
  1313.9 0.9 multiply_reduce_fusion.13
  1316.2 1.0 fusion.59
  1317.2 0.9 multiply_reduce_fusion.23
  1320.0 1.9 collective-permute-start.5
  1321.9 100.9 %all-reduce.3 = (f32[]{:T(128)}, f32[]{:T(128)}) all-reduce(f32[]{:T(128)S(6)} %add.349, f32[]{:T(128)S(6)} %add.355), channel_id=1, replica_groups=mesh['hours'=64,'region'=8] {'hours','region'}, use_global_device_ids=true, to_apply=%region_39.40 | all-reduce | flops 2 | bytes 16 | tf_op jit(solution)/shard_map/psum | solution.py:164
  1424.3 24.8 %all_gather.27 = f32[64,1024]{1,0:T(8,128)S(1)} all-gather(f32[64,128]{1,0:T(8,128)S(1)} %get-tuple-element.70), channel_id=1, replica_groups=mesh['hours'=64,'region'=8] {'region'}, dimensions={1}, use_global_device_ids=true | all-gather | bytes 294912 | tf_op jit(solution)/shard_map/all_gather | solution.py:85
  1449.5 1.6 subtract_reduce_fusion
  1451.0 0.7 fusion.69
  1452.1 1.3 fusion.68
  1455.2 32.9 %reduce-scatter.11.cloned.1.call-done = f32[64,128]{1,0:T(8,128)} async-done(((f32[64,1024]{1,0:T(8,128)}), f32[64,128]{1,0:T(8,128)}) %reduce-scatter.11.cloned.1.call-update) | async-done | bytes 32784 | tf_op jit(solution)/shard_map/reduce_scatter | solution.py:144
  1488.1 1.0 fusion.55
  1489.1 0.9 fusion.54
  (86 shorter events, 8.4 us)
Async XLA Ops:
  7.2 465.0 %reduce-scatter.5.cloned.1.call-start = ((), (), s32[]{:S(2)}) async-start(), calls=%async_computation.4 | async-start | bytes 294912 | tf_op jit(solution)/shard_map/reduce_scatter | solution.py:144
  7.9 2.1 copy-start.9
  7.9 461.4 %collective-permute-start = (f32[1,256]{1,0:T(1,128)S(1)}, f32[1,256]{1,0:T(1,128)S(1)}, u32[]{:S(2)}, u32[]{:S(2)}) collective-permute-start(f32[1,256]{1,0:T(1,128)S(1)} %bitcast.122), channel_id=1, source_target_pairs={{0,8},{8,16},{16,24},{24,32},{32,40},{40,48},{48,56},{56,64},{64,7... | collective-permute-start | bytes 3080 | tf_op jit(solution)/shard_map/ppermute | solution.py:14
  36.6 0.7 copy-start.13
  36.6 0.7 copy-start.12
  37.2 0.8 copy-start.1
  37.3 3.8 copy-start
  40.3 853.9 %reduce-scatter.7.cloned.1.call-start = ((), (), s32[]{:S(2)}) async-start(), calls=%async_computation.5 | async-start | bytes 294912 | tf_op jit(solution)/shard_map/reduce_scatter | solution.py:144
  40.3 0.7 copy-start.11
  40.3 0.7 copy-start.5
  40.4 0.7 copy-start.10
  181.0 0.7 copy-start.8
  314.0 11.8 copy-start.3
  340.6 126.1 %copy-start.7 = (f32[256]{0:T(256)S(1)}, f32[256]{0:T(256)}, u32[]{:S(2)}) copy-start(f32[256]{0:T(256)} %param.26) | copy-start | bytes 3076
  469.2 0.7 copy-start.4
  472.1 1.1 copy-start.2
  476.0 262.6 %collective-permute-start.1 = (f32[1,256]{1,0:T(1,128)S(1)}, f32[1,256]{1,0:T(1,128)S(1)}, u32[]{:S(2)}, u32[]{:S(2)}) collective-permute-start(f32[1,256]{1,0:T(1,128)S(1)} %slice.79), channel_id=1, source_target_pairs={{0,504},{8,0},{16,8},{24,16},{32,24},{40,32},{48,40},{56,48},{64,5... | collective-permute-start | bytes 3080 | tf_op jit(solution)/shard_map/ppermute | solution.py:14
  738.6 0.7 copy-start.6
  742.9 573.2 %reduce-scatter.9.cloned.1.call-start = ((), (), s32[]{:S(2)}) async-start(), calls=%async_computation.6 | async-start | bytes 294912 | tf_op jit(solution)/shard_map/reduce_scatter | solution.py:144
  756.0 135.9 %collective-permute-start.2 = (f32[1,256]{1,0:T(1,128)S(1)}, f32[1,256]{1,0:T(1,128)S(1)}, u32[]{:S(2)}, u32[]{:S(2)}) collective-permute-start(f32[1,256]{1,0:T(1,128)S(1)} %slice.80), channel_id=1, source_target_pairs={{0,8},{8,16},{16,24},{24,32},{32,40},{40,48},{48,56},{56,64},{64,7... | collective-permute-start | bytes 3080 | tf_op jit(solution)/shard_map/ppermute | solution.py:14
  898.0 130.7 %collective-permute-start.3 = (f32[1,256]{1,0:T(1,128)S(1)}, f32[1,256]{1,0:T(1,128)S(1)}, u32[]{:S(2)}, u32[]{:S(2)}) collective-permute-start(f32[1,256]{1,0:T(1,128)S(1)} %slice.83), channel_id=1, source_target_pairs={{0,504},{8,0},{16,8},{24,16},{32,24},{40,32},{48,40},{56,48},{64,5... | collective-permute-start | bytes 3080 | tf_op jit(solution)/shard_map/ppermute | solution.py:14
  1161.7 152.2 %collective-permute-start.4 = (f32[1,256]{1,0:T(1,128)S(1)}, f32[1,256]{1,0:T(1,128)S(1)}, u32[]{:S(2)}, u32[]{:S(2)}) collective-permute-start(f32[1,256]{1,0:T(1,128)S(1)} %slice.84), channel_id=1, source_target_pairs={{0,8},{8,16},{16,24},{24,32},{32,40},{40,48},{48,56},{56,64},{64,7... | collective-permute-start | bytes 3080 | tf_op jit(solution)/shard_map/ppermute | solution.py:14
  1166.6 321.5 %reduce-scatter.11.cloned.1.call-start = ((), (), s32[]{:S(2)}) async-start(), calls=%async_computation.7 | async-start | bytes 294912 | tf_op jit(solution)/shard_map/reduce_scatter | solution.py:144
  1320.0 134.3 %collective-permute-start.5 = (f32[1,256]{1,0:T(1,128)S(1)}, f32[1,256]{1,0:T(1,128)S(1)}, u32[]{:S(2)}, u32[]{:S(2)}) collective-permute-start(f32[1,256]{1,0:T(1,128)S(1)} %slice.87), channel_id=1, source_target_pairs={{0,504},{8,0},{16,8},{24,16},{32,24},{40,32},{48,40},{56,48},{64,5... | collective-permute-start | bytes 3080 | tf_op jit(solution)/shard_map/ppermute | solution.py:14
Sparse Core Ops, SparseCore 0:
  40.4 42.1 reduce-scatter.4
  743.0 39.1 reduce-scatter.6
  1166.7 41.5 reduce-scatter.8
  1453.5 34.5 reduce-scatter.10
where the time goes:
time: 1500 us
  blocking collectives  1280 us (85%)
  local copies, waits for them, and re-layouts  86.5 us (6%)
  between operations  36.6 us (2%)
  waiting for transfers between devices  33 us (2%)
  matrix products  26.5 us (2%)
  starting transfers between devices  16.8 us (1%)
  other arithmetic  16.8 us (1%)
    psum x4, blocking collectives, to_owners(): summed = lax.psum(partial_value, 'hours')  515 us
    unnamed x3, blocking collectives  367 us
    psum x3, blocking collectives, body(): dual_sum = lax.psum(dual_sq, ('hours', 'region'))  297 us
    all_gather x4, blocking collectives, body(): lax.all_gather(prices, 'region', axis=1, tiled=True)  101 us
    gather x3, local copies, waits for them, and re-layouts, body(): cap_dense = capacity_all[inverse].reshape(tech_count, node_count)  35.3 us
    gather x3, local copies, waits for them, and re-layouts, body(): jnp.sum(availability * cap_duals, axis=0).reshape(-1)[owner_cols]  35.3 us
    reduce_scatter x4, waiting for transfers between devices, body(): lax.psum_scatter(per_dest, 'region', scatter_dimension=1, tiled=True)  32.9 us
  transfers between devices with their start and end apart: 10, of which 1 were waited for; matrix products, arithmetic and copies ran while one was open for 7% of the time, Pallas kernels for 0%

commit v1 on v0

--- a/solution.py
+++ b/solution.py
@@ -161,7 +161,7 @@
                 + jnp.sum((cap_new - cap_duals) ** 2)
                 + jnp.sum((store_new - store_duals) ** 2)
             )
-            dual_sum = lax.psum(dual_sq, ("hours", "region"))
+            dual_sum = lax.psum(lax.psum(dual_sq, "hours"), "region")
             weight = jnp.sqrt(weight * jnp.sqrt((dual_sum + epsilon) / (primal_sum + epsilon)))
         dispatch, capacity, inner_flow, cross_flow = (
             dispatch_new,

time: 1500 us -> 1560 us (1.040)
  blocking collectives: 1280 us -> 1320 us
    psum x3 -> x7, blocking collectives: 297 us -> 467 us  [the longest x3 296 us: body(): primal_sum = lax.psum(primal_sq, ('hours', 'region'))]
    psum x4 -> x3, blocking collectives: 515 us -> 378 us  [to_owners(): summed = lax.psum(partial_value, 'hours')]
where the time goes in v1:
time: 1560 us; the launch traced here: 1550 us
  blocking collectives  1320 us (85%)
  local copies, waits for them, and re-layouts  86.5 us (6%)
  waiting for transfers between devices  36.7 us (2%)
  between operations  36.5 us (2%)
  starting transfers between devices  26.6 us (2%)
  matrix products  26.5 us (2%)
  other arithmetic  16.8 us (1%)
    unnamed x3, blocking collectives  379 us
    psum x3, blocking collectives, to_owners(): summed = lax.psum(partial_value, 'hours')  378 us
    psum x3, blocking collectives, body(): primal_sum = lax.psum(primal_sq, ('hours', 'region'))  296 us
    psum x4, blocking collectives, body(): dual_sum = lax.psum(lax.psum(dual_sq, 'hours'), 'region')  171 us
    all_gather x4, blocking collectives, body(): lax.all_gather(prices, 'region', axis=1, tiled=True)  101 us
    reduce_scatter x4, waiting for transfers between devices, body(): lax.psum_scatter(per_dest, 'region', scatter_dimension=1, tiled=True)  36.6 us
    gather x3, local copies, waits for them, and re-layouts, body(): cap_dense = capacity_all[inverse].reshape(tech_count, node_count)  35.3 us
    gather x3, local copies, waits for them, and re-layouts, body(): jnp.sum(availability * cap_duals, axis=0).reshape(-1)[owner_cols]  35.3 us
  transfers between devices with their start and end apart: 10, of which 1 were waited for; matrix products, arithmetic and copies ran while one was open for 7% of the time, Pallas kernels for 0%

profile of v1, /device:TPU:2, one launch (start us, length us, event | category | flops | bytes accessed | tf_op | source)
XLA Modules:
  0.0 1554.0 jit_solution(18008598042695098387)
XLA Ops:
  7.2 0.7 broadcast_minimum_fusion
  7.9 2.0 collective-permute-start
  10.0 26.6 %all_gather.21 = f32[64,1024]{1,0:T(8,128)S(1)} all-gather(f32[64,128]{1,0:T(8,128)} %param.27), channel_id=1, replica_groups=mesh['hours'=64,'region'=8] {'region'}, dimensions={1}, use_global_device_ids=true | all-gather | bytes 294912 | tf_op jit(solution)/shard_map/all_gather | solution.py:85
  37.3 0.7 fusion.75
  38.1 0.9 multiply_reduce_fusion.20
  39.0 1.3 fusion.74
  41.2 11.8 gather_fusion
  53.0 126.8 %psum.91 = f32[2048]{0:T(1024)S(1)} all-reduce(f32[2048]{0:T(1024)S(1)} %gather_fusion), channel_id=1, replica_groups=mesh['hours'=64,'region'=8] {'hours'}, use_global_device_ids=true, to_apply=%region_5.6 | all-reduce | flops 2048 | bytes 16384 | tf_op jit(solution)/shard_map/psum | solution.py:22
  179.7 1.3 dynamic-slice
  181.7 0.7 multiply_reduce_fusion.28
  182.5 126.4 %all-reduce = f32[2048]{0:T(1024)S(1)} all-reduce(f32[2048]{0:T(1024)S(1)} %multiply_dynamic-update-slice_fusion), channel_id=1, replica_groups=mesh['hours'=64,'region'=8] {'hours'}, use_global_device_ids=true, to_apply=%add | all-reduce | flops 2048 | bytes 16384
  308.9 5.0 sort.17
  314.0 11.8 gather_fusion.1
  325.8 1.1 multiply_reduce_fusion.6
  326.8 1.0 multiply_reduce_fusion.21
  328.8 11.8 gather_fusion.2
  343.8 0.9 multiply_reduce_fusion.19
  346.0 6.6 collective-permute-start.1
  352.6 95.6 %psum.94 = f32[]{:T(128)} all-reduce(f32[]{:T(128)S(6)} %add.321), channel_id=1, replica_groups=mesh['hours'=64,'region'=8] {'hours','region'}, use_global_device_ids=true, to_apply=%region_17.18 | all-reduce | flops 1 | bytes 8 | tf_op jit(solution)/shard_map/psum | solution.py:130
  448.9 1.0 fusion.67
  449.9 0.9 multiply_reduce_fusion.25
  452.7 126.3 %all-reduce.5 = (f32[2048]{0:T(1024)S(1)}, f32[]{:T(128)}) all-reduce(f32[2048]{0:T(1024)S(1)} %gather_fusion.2, f32[]{:T(128)S(6)} %add.315), channel_id=1, replica_groups=mesh['hours'=64,'region'=8] {'hours'}, use_global_device_ids=true, to_apply=%region_22.23 | all-reduce | flops 2049 | bytes 16392 | tf_op jit(solution)/shard_map/psum | solution.py:22
  579.0 14.8 psum.93
  594.6 24.8 %all_gather.23 = f32[64,1024]{1,0:T(8,128)S(1)} all-gather(f32[64,128]{1,0:T(8,128)S(1)} %get-tuple-element.56), channel_id=1, replica_groups=mesh['hours'=64,'region'=8] {'region'}, dimensions={1}, use_global_device_ids=true | all-gather | bytes 294912 | tf_op jit(solution)/shard_map/all_gather | solution.py:85
  619.5 1.0 multiply_reduce_fusion.17
  621.3 126.1 %all-reduce.1 = f32[2048]{0:T(1024)S(1)} all-reduce(f32[2048]{0:T(1024)S(1)} %subtract_dynamic-update-slice_fusion.1), channel_id=1, replica_groups=mesh['hours'=64,'region'=8] {'hours'}, use_global_device_ids=true, to_apply=%add.1 | all-reduce | flops 2048 | bytes 16384
  747.4 11.8 gather_fusion.3
  760.6 1.9 collective-permute-start.2
  762.5 0.7 fusion.73
  763.2 0.9 multiply_reduce_fusion.16
  764.1 1.3 fusion.72
  765.5 1.2 multiply_reduce_fusion.3
  767.0 11.8 gather_fusion.4
  781.4 1.0 multiply_reduce_fusion.15
  783.6 7.0 collective-permute-start.3
  790.6 100.1 %psum.98 = f32[]{:T(128)} all-reduce(f32[]{:T(128)S(6)} %add.341), channel_id=1, replica_groups=mesh['hours'=64,'region'=8] {'hours','region'}, use_global_device_ids=true, to_apply=%region_33.34 | all-reduce | flops 1 | bytes 8 | tf_op jit(solution)/shard_map/psum | solution.py:130
  891.4 1.0 fusion.63
  892.4 0.9 multiply_reduce_fusion.24
  895.2 124.9 %all-reduce.4 = (f32[2048]{0:T(1024)S(1)}, f32[]{:T(128)}) all-reduce(f32[2048]{0:T(1024)S(1)} %gather_fusion.4, f32[]{:T(128)S(6)} %add.335), channel_id=1, replica_groups=mesh['hours'=64,'region'=8] {'hours'}, use_global_device_ids=true, to_apply=%region_38.39 | all-reduce | flops 2049 | bytes 16392 | tf_op jit(solution)/shard_map/psum | solution.py:22
  1020.1 15.9 %psum.97 = f32[]{:T(128)} all-reduce(f32[]{:T(128)} %get-tuple-element.25), channel_id=1, replica_groups=mesh['hours'=64,'region'=8] {'region'}, use_global_device_ids=true, to_apply=%region_26.27 | all-reduce | flops 1 | bytes 8 | tf_op jit(solution)/shard_map/psum | solution.py:164
  1037.5 1.0 multiply_reduce_fusion.12
  1038.6 24.8 %all_gather.25 = f32[64,1024]{1,0:T(8,128)S(1)} all-gather(f32[64,128]{1,0:T(8,128)S(1)} %get-tuple-element.63), channel_id=1, replica_groups=mesh['hours'=64,'region'=8] {'region'}, dimensions={1}, use_global_device_ids=true | all-gather | bytes 294912 | tf_op jit(solution)/shard_map/all_gather | solution.py:85
  1064.1 126.1 %all-reduce.2 = f32[2048]{0:T(1024)S(1)} all-reduce(f32[2048]{0:T(1024)S(1)} %subtract_dynamic-update-slice_fusion), channel_id=1, replica_groups=mesh['hours'=64,'region'=8] {'hours'}, use_global_device_ids=true, to_apply=%add.2 | all-reduce | flops 2048 | bytes 16384
  1190.3 11.8 gather_fusion.5
  1202.1 1.9 collective-permute-start.4
  1204.0 0.7 fusion.71
  1204.7 0.9 multiply_reduce_fusion.11
  1205.6 1.3 fusion.70
  1207.0 1.4 multiply_reduce_fusion
  1208.8 11.8 gather_fusion.6
  1223.1 0.9 multiply_reduce_fusion.13
  1225.3 7.0 collective-permute-start.5
  1232.3 100.0 %psum.102 = f32[]{:T(128)} all-reduce(f32[]{:T(128)S(6)} %add.361), channel_id=1, replica_groups=mesh['hours'=64,'region'=8] {'hours','region'}, use_global_device_ids=true, to_apply=%region_49.50 | all-reduce | flops 1 | bytes 8 | tf_op jit(solution)/shard_map/psum | solution.py:130
  1332.3 1.0 fusion.59
  1333.3 0.9 multiply_reduce_fusion.23
  1336.7 124.9 %all-reduce.3 = (f32[]{:T(128)}, f32[2048]{0:T(1024)S(1)}) all-reduce(f32[]{:T(128)S(6)} %add.355, f32[2048]{0:T(1024)S(1)} %gather_fusion.6), channel_id=1, replica_groups=mesh['hours'=64,'region'=8] {'hours'}, use_global_device_ids=true, to_apply=%region_41.42 | all-reduce | flops 2049 | bytes 16392 | tf_op jit(solution)/shard_map/psum | solution.py:164
  1461.6 15.7 %psum.101 = f32[]{:T(128)} all-reduce(f32[]{:T(128)} %get-tuple-element.22), channel_id=1, replica_groups=mesh['hours'=64,'region'=8] {'region'}, use_global_device_ids=true, to_apply=%region_42.43 | all-reduce | flops 1 | bytes 8 | tf_op jit(solution)/shard_map/psum | solution.py:164
  1478.1 24.8 %all_gather.27 = f32[64,1024]{1,0:T(8,128)S(1)} all-gather(f32[64,128]{1,0:T(8,128)S(1)} %get-tuple-element.70), channel_id=1, replica_groups=mesh['hours'=64,'region'=8] {'region'}, dimensions={1}, use_global_device_ids=true | all-gather | bytes 294912 | tf_op jit(solution)/shard_map/all_gather | solution.py:85
  1503.3 1.6 subtract_reduce_fusion
  1504.9 0.7 fusion.69
  1505.9 1.3 fusion.68
  1509.1 36.6 %reduce-scatter.11.cloned.1.call-done = f32[64,128]{1,0:T(8,128)} async-done(((f32[64,1024]{1,0:T(8,128)}), f32[64,128]{1,0:T(8,128)}) %reduce-scatter.11.cloned.1.call-update) | async-done | bytes 32784 | tf_op jit(solution)/shard_map/reduce_scatter | solution.py:144
  1545.6 1.0 fusion.55
  1546.6 0.9 fusion.54
  (89 shorter events, 10.4 us)
Async XLA Ops:
  7.2 441.7 %reduce-scatter.5.cloned.1.call-start = ((), (), s32[]{:S(2)}) async-start(), calls=%async_computation.4 | async-start | bytes 294912 | tf_op jit(solution)/shard_map/reduce_scatter | solution.py:144
  7.9 2.1 copy-start.9
  7.9 335.2 %collective-permute-start = (f32[1,256]{1,0:T(1,128)S(1)}, f32[1,256]{1,0:T(1,128)S(1)}, u32[]{:S(2)}, u32[]{:S(2)}) collective-permute-start(f32[1,256]{1,0:T(1,128)S(1)} %bitcast.122), channel_id=1, source_target_pairs={{0,8},{8,16},{16,24},{24,32},{32,40},{40,48},{48,56},{56,64},{64,7... | collective-permute-start | bytes 3080 | tf_op jit(solution)/shard_map/ppermute | solution.py:14
  36.6 0.7 copy-start.13
  36.6 0.7 copy-start.12
  37.2 0.8 copy-start.1
  37.3 3.8 copy-start
  40.3 851.1 %reduce-scatter.7.cloned.1.call-start = ((), (), s32[]{:S(2)}) async-start(), calls=%async_computation.5 | async-start | bytes 294912 | tf_op jit(solution)/shard_map/reduce_scatter | solution.py:144
  40.3 0.7 copy-start.11
  40.3 0.7 copy-start.5
  40.4 0.7 copy-start.10
  181.0 0.7 copy-start.8
  314.0 11.8 copy-start.3
  328.1 0.7 copy-start.7
  343.1 0.7 copy-start.4
  346.0 413.2 %collective-permute-start.1 = (f32[1,256]{1,0:T(1,128)S(1)}, f32[1,256]{1,0:T(1,128)S(1)}, u32[]{:S(2)}, u32[]{:S(2)}) collective-permute-start(f32[1,256]{1,0:T(1,128)S(1)} %slice.79), channel_id=1, source_target_pairs={{0,504},{8,0},{16,8},{24,16},{32,24},{40,32},{48,40},{56,48},{64,5... | collective-permute-start | bytes 3080 | tf_op jit(solution)/shard_map/ppermute | solution.py:14
  448.9 1.1 copy-start.2
  759.2 0.7 copy-start.6
  760.6 20.8 %collective-permute-start.2 = (f32[1,256]{1,0:T(1,128)S(1)}, f32[1,256]{1,0:T(1,128)S(1)}, u32[]{:S(2)}, u32[]{:S(2)}) collective-permute-start(f32[1,256]{1,0:T(1,128)S(1)} %slice.80), channel_id=1, source_target_pairs={{0,8},{8,16},{16,24},{24,32},{32,40},{40,48},{48,56},{56,64},{64,7... | collective-permute-start | bytes 3080 | tf_op jit(solution)/shard_map/ppermute | solution.py:14
  765.4 566.8 %reduce-scatter.9.cloned.1.call-start = ((), (), s32[]{:S(2)}) async-start(), calls=%async_computation.6 | async-start | bytes 294912 | tf_op jit(solution)/shard_map/reduce_scatter | solution.py:144
  783.6 279.7 %collective-permute-start.3 = (f32[1,256]{1,0:T(1,128)S(1)}, f32[1,256]{1,0:T(1,128)S(1)}, u32[]{:S(2)}, u32[]{:S(2)}) collective-permute-start(f32[1,256]{1,0:T(1,128)S(1)} %slice.83), channel_id=1, source_target_pairs={{0,504},{8,0},{16,8},{24,16},{32,24},{40,32},{48,40},{56,48},{64,5... | collective-permute-start | bytes 3080 | tf_op jit(solution)/shard_map/ppermute | solution.py:14
  1202.1 21.0 %collective-permute-start.4 = (f32[1,256]{1,0:T(1,128)S(1)}, f32[1,256]{1,0:T(1,128)S(1)}, u32[]{:S(2)}, u32[]{:S(2)}) collective-permute-start(f32[1,256]{1,0:T(1,128)S(1)} %slice.84), channel_id=1, source_target_pairs={{0,8},{8,16},{16,24},{24,32},{32,40},{40,48},{48,56},{56,64},{64,7... | collective-permute-start | bytes 3080 | tf_op jit(solution)/shard_map/ppermute | solution.py:14
  1207.0 338.7 %reduce-scatter.11.cloned.1.call-start = ((), (), s32[]{:S(2)}) async-start(), calls=%async_computation.7 | async-start | bytes 294912 | tf_op jit(solution)/shard_map/reduce_scatter | solution.py:144
  1225.3 282.8 %collective-permute-start.5 = (f32[1,256]{1,0:T(1,128)S(1)}, f32[1,256]{1,0:T(1,128)S(1)}, u32[]{:S(2)}, u32[]{:S(2)}) collective-permute-start(f32[1,256]{1,0:T(1,128)S(1)} %slice.87), channel_id=1, source_target_pairs={{0,504},{8,0},{16,8},{24,16},{32,24},{40,32},{48,40},{56,48},{64,5... | collective-permute-start | bytes 3080 | tf_op jit(solution)/shard_map/ppermute | solution.py:14
Sparse Core Ops, SparseCore 0:
  40.4 42.1 reduce-scatter.4
  765.6 40.8 reduce-scatter.6
  1207.1 40.5 reduce-scatter.8
  1507.3 38.2 reduce-scatter.10
